TPU v7x, 32 devices: a whole 2x2x4 slice. The times are simulated.
32 devices in a mesh: re: 2 (over x), rp: 8 (over z, core), mode: 2 (over y).
Axes of the slice: x: 2, y: 2, z: 4, core: 2. Of those that a mesh axis runs over, the one named last changes fastest.
Arguments:
- coupling: float32 [2, 16, 8, 120, 576], P(None, 're', 'rp', 'mode'), may hold values from -0.5 to 0.5
- electron_cells: int32 [16, 3], replicated, may hold values from -6 to 6
- phonon_cells: int32 [8, 3], replicated, may hold values from -3 to 3
- kpoint_index: int32 [4, 3], replicated, may hold values from 0 to 15
- qpoint_index: int32 [8, 3], replicated, may hold values from 0 to 15
- eigenvectors: float32 [8, 2, 120, 120], P('rp', None, 'mode'), may hold values from -0.5 to 0.5
- frequencies: float32 [8, 120], P('rp', 'mode'), may hold values from 0.25 to 2
Outputs:
- mode_coupling: float32 [120, 8, 4, 2, 576], P('mode', 'rp', 're')
All inputs are finite; a program needn't handle non-finite values.
Results may differ from a plain program's by a relative error of at most 0.00007.
Values sent between devices are 32-bit elements; how exact they have to be, the bound alone decides.
A program may use at most 64 MiB of HBM per device.

v0:
```python
import jax
import jax.numpy as jnp
from jax import lax
from jax.sharding import PartitionSpec as P

KG = 16


def phases(points, cells):
    turns = jnp.sum(points[:, None, :] * cells[None, :, :], axis=-1) % KG
    angle = turns.astype(jnp.float32) * (2.0 * 3.141592653589793 / KG)
    return (jnp.cos(angle), jnp.sin(angle))


def complex_rows(cos_t, sin_t):
    count = cos_t.shape[0]
    upper = jnp.stack([cos_t, -sin_t], axis=1)
    lower = jnp.stack([sin_t, cos_t], axis=1)
    return jnp.stack([upper, lower], axis=1).reshape(count * 2, 2 * cos_t.shape[1])


def electron_apply(cos_t, sin_t, block):
    rows = block.shape[1]
    rest = block.shape[2:]
    flat = block.reshape(2 * rows, -1)
    summed = jnp.dot(complex_rows(cos_t, sin_t), flat, precision=lax.Precision.HIGHEST)
    return summed.reshape((cos_t.shape[0], 2) + rest)


def phonon_apply(cos_t, sin_t, block):
    hp = lax.Precision.HIGHEST
    swapped = jnp.concatenate([-block[:, 1:2], block[:, 0:1]], axis=1)
    first_term = jnp.einsum("qs,kbsx->qkbx", cos_t, block, precision=hp)
    second_term = jnp.einsum("qs,kbsx->qkbx", sin_t, swapped, precision=hp)
    return first_term + second_term


def shards(
    coupling, electron_cells, phonon_cells, kpoint_index, qpoint_index, eigenvectors, frequencies
):
    hp = lax.Precision.HIGHEST
    re_local = coupling.shape[1]
    rp_local = coupling.shape[2]
    modes_local = coupling.shape[3]
    pairs = coupling.shape[4]
    k_local = kpoint_index.shape[0] // lax.axis_size("re")
    q_local = qpoint_index.shape[0] // lax.axis_size("rp")
    columns = coupling.reshape(2, re_local, rp_local, modes_local * pairs)
    my_electron = lax.dynamic_slice_in_dim(
        electron_cells, lax.axis_index("re") * re_local, re_local, 0
    )
    points = kpoint_index
    cos_e, sin_e = phases(points, my_electron)
    bloch_k = lax.psum_scatter(
        electron_apply(cos_e, sin_e, columns), "re", scatter_dimension=0, tiled=True
    )
    my_phonon = lax.dynamic_slice_in_dim(phonon_cells, lax.axis_index("rp") * rp_local, rp_local, 0)
    points = qpoint_index
    cos_p, sin_p = phases(points, my_phonon)
    bloch_kq = lax.psum_scatter(
        phonon_apply(cos_p, sin_p, bloch_k), "rp", scatter_dimension=0, tiled=True
    )
    bloch_kq = bloch_kq.reshape(q_local, k_local, 2, modes_local, pairs)
    contract = (((0,), (2,)), ((), ()))
    kq_one = bloch_kq[0]
    swapped = jnp.concatenate([-kq_one[:, 1:2], kq_one[:, 0:1]], axis=1)
    vec_real = eigenvectors[0, 0]
    vec_imag = eigenvectors[0, 1]
    part_one = lax.dot_general(vec_real, kq_one, contract, precision=hp)
    part_two = lax.dot_general(vec_imag, swapped, contract, precision=hp)
    results = [part_one + part_two]
    rotated = lax.psum_scatter(jnp.stack(results, axis=1), "mode", scatter_dimension=0, tiled=True)
    factor = lax.rsqrt(2.0 * frequencies).T[:, :, None, None, None]
    return rotated * factor


def solution(mesh):
    placed = (
        P(None, "re", "rp", "mode", None),
        P(),
        P(),
        P(),
        P(),
        P("rp", None, "mode", None),
        P("rp", "mode"),
    )
    return jax.shard_map(
        shards,
        mesh=mesh,
        in_specs=placed,
        out_specs=P("mode", "rp", "re", None, None),
        check_vma=False,
    )
```

profile of v0, /device:TPU:0, one launch (start us, length us, event | category | flops | bytes accessed | tf_op | source)
XLA Modules:
  0.0 235.2 jit_solution(8280663059204704020)
XLA Ops:
  6.5 0.8 copy.32
  7.7 7.8 %reduce.3 = f32[2,8,60,576]{3,2,1,0:T(8,128)S(1)} reduce(f32[2,8,1,60,576]{4,2,3,1,0:T(1,128)} %param.7, f32[]{:T(128)} %constant.57), dimensions={2}, to_apply=%param.7.reduce_sub_computation | reduce | bytes 4423684 | tf_op args[0]
  15.5 2.2 reshape.124
  17.8 4.3 %convolution_bitcast_fusion = f32[4,2,1,34560]{3,0,1,2:T(4,128)} fusion(f32[16,34560,1]{1,0,2:T(8,128)} %reshape.124, f32[4,1,16]{2,0,1:T(4,128)S(1)} %stack.25, f32[4,1,16]{2,0,1:T(4,128)S(1)} %stack.23), kind=kOutput, calls=%fused_computation | convolution fusion | flops 53084288 | bytes 3318272 | tf_op jit(solution)/shard_map/dot_general | solution.py:26
  22.1 0.2 all-reduce.9.cloned.1.call-start
  22.7 0.6 dynamic-slice
  24.0 42.3 %all-reduce.7.cloned.1.call-done = f32[4,2,1,34560]{3,0,1,2:T(4,128)} async-done(((f32[4,2,1,34560]{3,0,1,2:T(4,128)}), f32[4,2,1,34560]{3,0,1,2:T(4,128)}) %all-reduce.7.cloned.1.call-update) | async-done | bytes 1105936
  66.3 1.6 dynamic-slice_negate_fusion
  67.9 0.2 maximum_bitcast_fusion
  68.1 0.3 copy.36
  68.4 0.2 dynamic-slice_bitcast_fusion
  68.7 0.3 copy.35
  69.0 4.0 %multiply_add_fusion = f32[8,2,2,34560]{3,2,1,0:T(2,128)} fusion(f32[2,2,34560]{2,1,0:T(2,128)S(1)} %copy.36, f32[2,2,34560]{2,1,0:T(2,128)S(1)} %copy.35, f32[8]{0:T(128)S(1)} %sin.25, f32[8]{0:T(128)S(1)} %get-tuple-element.5), kind=kLoop, calls=%fused_computation.1 | loop fusion | flops 3317760 | bytes 5529664 | tf_op jit(solution)/shard_map/add | solution.py:35
  73.0 0.6 copy-done.7
  73.6 0.6 dynamic-slice.2
  74.2 100.3 %all-reduce.9.cloned.1.call-done = f32[8,2,2,34560]{3,2,1,0:T(2,128)} async-done(((f32[8,2,2,34560]{3,2,1,0:T(2,128)}), f32[8,2,2,34560]{3,2,1,0:T(2,128)}) %all-reduce.9.cloned.1.call-update) | async-done | bytes 4423696
  174.6 1.7 constant_dynamic-slice_fusion.1
  176.3 0.6 squeeze_reshape.3
  177.0 2.0 fusion.4
  179.0 2.0 fusion
  181.1 1.4 copy.39
  182.5 0.6 dynamic-slice.4
  183.8 42.7 %all-reduce.11.cloned.1.call-done = f32[120,1,2,2,576]{4,3,2,1,0:T(2,128)} async-done(((f32[120,1,2,2,576]{4,3,2,1,0:T(2,128)}), f32[120,1,2,2,576]{4,3,2,1,0:T(2,128)}) %all-reduce.11.cloned.1.call-update) | async-done | bytes 1105936
  226.5 2.2 dynamic-slice_multiply_fusion
  (37 shorter events, 1.0 us)
Async XLA Ops:
  6.5 0.8 copy-start
  6.5 59.8 %all-reduce.7.cloned.1.call-start = ((), (), s32[]{:S(2)}) async-start(), calls=%async_computation | async-start | bytes 2211840
  17.8 4.6 %copy-start.3 = (s32[8,3]{0,1:T(4,128)S(1)}, s32[8,3]{0,1:T(4,128)}, u32[]{:S(2)}) copy-start(s32[8,3]{0,1:T(4,128)} %param.9) | copy-start | bytes 292
  17.8 4.8 %copy-start.4 = (s32[8,3]{0,1:T(4,128)S(1)}, s32[8,3]{0,1:T(4,128)}, u32[]{:S(2)}) copy-start(s32[8,3]{0,1:T(4,128)} %param.11) | copy-start | bytes 292
  17.8 5.0 %copy-start.8 = (u32[32]{0:T(128)S(1)}, u32[32]{0:T(128)}, u32[]{:S(2)}) copy-start(u32[32]{0:T(128)} %constant.46) | copy-start | bytes 388
  22.1 152.5 %all-reduce.9.cloned.1.call-start = ((), (), s32[]{:S(2)}) async-start(), calls=%async_computation.1 | async-start | bytes 8847360
  66.3 2.1 copy-start.1
  72.9 0.7 copy-start.7
  72.9 1.2 copy-start.2
  73.0 153.6 %all-reduce.11.cloned.1.call-start = ((), (), s32[]{:S(2)}) async-start(), calls=%async_computation.2 | async-start | bytes 2457600
  181.0 1.5 copy-start.6
  181.1 2.7 %copy-start.5 = (f32[1,60]{1,0:T(1,128)S(1)}, f32[1,60]{1,0:T(1,128)}, u32[]{:S(2)}) copy-start(f32[1,60]{1,0:T(1,128)} %param.13) | copy-start | bytes 724
Sparse Core Ops, SparseCore 0:
  22.2 44.0 all-reduce.6
  73.1 101.4 all-reduce.8
  182.6 43.8 all-reduce.10
where the time goes:
time: 236 us; the launch traced here: 235 us
  waiting for transfers between devices  185 us (78%)
  other arithmetic  16.1 us (7%)
  between operations  14.6 us (6%)
  local copies, waits for them, and re-layouts  10.4 us (4%)
  matrix products  8.36 us (4%)
    unnamed x6, waiting for transfers between devices  185 us
    unnamed x1, other arithmetic  7.82 us
    unnamed x23, local copies, waits for them, and re-layouts  4.88 us
  transfers between devices with their start and end apart: 3, of which 3 were waited for; matrix products, arithmetic and copies ran while one was open for 1% of the time, Pallas kernels for 0%

commit v1 on v0

v1 whole, which is shorter than its diff:
```python
import functools

import jax
import jax.numpy as jnp
from jax import lax
from jax.experimental import pallas as pl
from jax.experimental.pallas import tpu as pltpu
from jax.sharding import PartitionSpec as P

KG = 16
CORES = 2
LANES = 128
CHUNKS = 3
MESH = pl.DeviceIdType.MESH


def phases(points, cells):
    turns = jnp.sum(points[:, None, :] * cells[None, :, :], axis=-1) % KG
    angle = turns.astype(jnp.float32) * (2.0 * 3.141592653589793 / KG)
    return (jnp.cos(angle), jnp.sin(angle))


def row_blocks(rows, step):
    return [(r, min(r + step, rows)) for r in range(0, rows, step)]


def pieces_of(chunk, width, pairs):
    found = []
    at = chunk * width
    end = at + width
    while at < end:
        k = at // pairs
        stop = min(end, (k + 1) * pairs)
        found.append((k, at - k * pairs, stop - k * pairs, at - chunk * width))
        at = stop
    return found


def kernel(
    sizes, coupling, cos_e, sin_e, cos_p, sin_p, turn, out,
    xout, xin, raw, sumout, sumin, mine, sibout, sibin, packed, yout, yin,
    xs, xr, rs, rr, ss, sr, bs, br, ys, yr,
):
    n_re, n_rp, n_mode, chunks, width = sizes
    re_local, modes, pairs = coupling.shape[1], coupling.shape[3], coupling.shape[4]
    k_local = out.shape[0]
    pad = raw.shape[3]
    half = n_rp // CORES // 2
    me_re, me_rp, me_mode = lax.axis_index("re"), lax.axis_index("rp"), lax.axis_index("mode")
    chip, core = me_rp // CORES, me_rp % CORES
    side = jnp.where(chip >= half, 1, 0)
    depth = jnp.where(side == 1, chip - half, half - 1 - chip)

    def chip_at(d, s):
        return jnp.where(s == 1, half + d, half - 1 - d)

    inner = jnp.where(depth == 0, chip_at(0, 1 - side), chip_at(depth - 1, side)) * CORES + core
    outer = chip_at(jnp.minimum(depth + 1, half - 1), side) * CORES + core
    sibling = chip * CORES + 1 - core
    re_peers = [lax.rem(me_re + d, n_re) for d in range(1, n_re)]
    mode_peers = [lax.rem(me_mode + d, n_mode) for d in range(1, n_mode)]

    def remote(src, dst, send, recv, where):
        return pltpu.make_async_remote_copy(
            src_ref=src, dst_ref=dst, send_sem=send, recv_sem=recv,
            device_id=where, device_id_type=MESH,
        )

    def x_copy(d, j):
        return remote(xout.at[d, j], xin.at[d, j], xs.at[d, j], xr.at[d, j], {"re": re_peers[d]})

    def raw_copy(tt, i, j):
        to = half + i if tt == 0 else i + 1
        return remote(raw.at[i, j], raw.at[to, j], rs.at[i, j], rr.at[to, j], {"rp": inner})

    def raw_arrival(i, j):
        return remote(raw.at[i, j], raw.at[i, j], rs.at[0, j], rr.at[i, j], {"rp": inner})

    def sum_copy(i, c, j):
        return remote(
            sumout.at[i, c, j], sumin.at[i, c, j], ss.at[i, c, j], sr.at[i, c, j], {"rp": outer}
        )

    def sum_arrival(i, c, j):
        return remote(
            sumin.at[i, c, j], sumin.at[i, c, j], ss.at[0, c, j], sr.at[i, c, j], {"rp": outer}
        )

    def sib_copy(j):
        return remote(sibout.at[j], sibin.at[j], bs.at[j], br.at[j], {"rp": sibling})

    def y_copy(d, j):
        return remote(
            yout.at[mode_peers[d], j], yin.at[d, j], ys.at[d, j], yr.at[d, j],
            {"mode": mode_peers[d]},
        )

    barrier = pltpu.get_barrier_semaphore()

    def greet(where):
        pl.semaphore_signal(barrier, inc=1, device_id=where, device_id_type=MESH)

    for p in re_peers:
        greet({"re": p})
    for p in mode_peers:
        greet({"mode": p})
    greet({"rp": sibling})
    greet({"rp": inner})

    @pl.when(depth < half - 1)
    def _():
        greet({"rp": outer})

    friends = n_re - 1 + n_mode - 1 + 2
    pl.semaphore_wait(barrier, friends + jnp.where(depth < half - 1, 1, 0))

    def electron(owner, j, dst):
        for k, p0, p1, at in pieces_of(j, width, pairs):
            row = owner * k_local + k
            for r0, r1 in row_blocks(modes, 32):
                real = imag = None
                for r in range(re_local):
                    col = me_re * re_local + r
                    c, s = cos_e[row, col], sin_e[row, col]
                    a = coupling[0, r, 0, r0:r1, p0:p1]
                    b = coupling[1, r, 0, r0:r1, p0:p1]
                    x, y = c * a - s * b, c * b + s * a
                    real = x if real is None else real + x
                    imag = y if imag is None else imag + y
                dst[0, r0:r1, at:at + p1 - p0] = real
                dst[1, r0:r1, at:at + p1 - p0] = imag

    def phonon(dst, q, terms, start):
        for r0, r1 in row_blocks(modes, 32):
            real = imag = None
            if start is not None:
                real, imag = start[0, r0:r1, :], start[1, r0:r1, :]
            for src, s_chip in terms:
                s_at = s_chip * CORES + core
                c, s = cos_p[q, s_at], sin_p[q, s_at]
                a, b = src[0, r0:r1, :], src[1, r0:r1, :]
                x, y = c * a - s * b, c * b + s * a
                real = x if real is None else real + x
                imag = y if imag is None else imag + y
            dst[0, r0:r1, :] = real
            dst[1, r0:r1, :] = imag

    for j in range(chunks):
        for d in range(n_re - 1):
            electron(re_peers[d], j, xout.at[d, j])
            x_copy(d, j).start()
    for j in range(chunks):
        electron(me_re, j, raw.at[0, j])
    packed[...] = jnp.zeros_like(packed)

    def x_stage(j):
        for d in range(n_re - 1):
            x_copy(d, j).wait_recv()
        for r0, r1 in row_blocks(modes, 32):
            for part in range(2):
                total = raw[0, j, part, r0:r1, :]
                for d in range(n_re - 1):
                    total = total + xin[d, j, part, r0:r1, :]
                raw[0, j, part, r0:r1, :] = total
        for tt in range(half):
            @pl.when(depth == tt)
            def _():
                raw_copy(tt, 0, j).start()

    def forward_stage(j):
        for tt in range(half - 1):
            @pl.when(depth == tt)
            def _():
                for i in range(1, half - tt):
                    raw_arrival(i, j).wait_recv()
                    raw_copy(tt, i, j).start()

    def z_stage(j):
        for tt in range(half):
            @pl.when(depth == tt)
            def _():
                own = (raw.at[0, j], chip)
                outside = [(raw.at[i, j], chip_at(tt + i, side)) for i in range(1, half - tt)]
                if tt == 0:
                    for i in range(half):
                        raw_arrival(half + i, j).wait_recv()
                    across = [(raw.at[half + i, j], chip_at(i, 1 - side)) for i in range(half)]
                else:
                    for i in range(half - tt):
                        for c in range(CORES):
                            sum_arrival(i, c, j).wait_recv()
                    across = []
                for i in range(half - 1 - tt):
                    for c in range(CORES):
                        q = chip_at(tt + 1 + i, side) * CORES + c
                        start = None if tt == 0 else sumin.at[i + 1, c, j]
                        phonon(sumout.at[i, c, j], q, [own] + across, start)
                        sum_copy(i, c, j).start()
                for dst, c in ((sibout, 1 - core), (mine, core)):
                    start = None if tt == 0 else sumin.at[0, c, j]
                    phonon(dst.at[j], chip * CORES + c, [own] + across + outside, start)
                    if dst is sibout:
                        sib_copy(j).start()

    def mode_stage(j):
        sib_copy(j).wait_recv()
        for part in range(2):
            packed[part * pad:part * pad + modes, :] = (
                mine[j, part, :modes, :] + sibin[j, part, :modes, :]
            )
        turned = jnp.dot(
            turn[...], packed[...], precision=lax.Precision.HIGHEST,
            preferred_element_type=jnp.float32,
        )
        yout[:, j] = turned.reshape(n_mode, 2, pad, width)
        for d in range(n_mode - 1):
            y_copy(d, j).start()

    def out_stage(j):
        for d in range(n_mode - 1):
            y_copy(d, j).wait_recv()
        for part in range(2):
            total = yout[me_mode, j, part]
            for d in range(n_mode - 1):
                total = total + yin[d, j, part]
            for k, p0, p1, at in pieces_of(j, width, pairs):
                out[k, part, :, p0:p1] = total[:modes, at:at + p1 - p0]

    for j in range(chunks + 1):
        if j < chunks:
            x_stage(j)
        if j >= 1:
            forward_stage(j - 1)
    for j in range(chunks + 2):
        if j < chunks:
            z_stage(j)
        if 1 <= j <= chunks:
            mode_stage(j - 1)
        if j >= 2:
            out_stage(j - 2)

    for j in range(chunks):
        for d in range(n_re - 1):
            x_copy(d, j).wait_send()
        sib_copy(j).wait_send()
        for d in range(n_mode - 1):
            y_copy(d, j).wait_send()
        for tt in range(half):
            @pl.when(depth == tt)
            def _():
                for i in range(half - tt):
                    raw_copy(tt, i, j).wait_send()
                for i in range(half - 1 - tt):
                    for c in range(CORES):
                        sum_copy(i, c, j).wait_send()


def shards(
    coupling, electron_cells, phonon_cells, kpoint_index, qpoint_index, eigenvectors, frequencies
):
    n_re, n_rp, n_mode = lax.axis_size("re"), lax.axis_size("rp"), lax.axis_size("mode")
    modes, pairs = coupling.shape[3], coupling.shape[4]
    k_local = kpoint_index.shape[0] // n_re
    columns = k_local * pairs
    chunks = CHUNKS if columns % (CHUNKS * LANES) == 0 else 1
    width = columns // chunks
    pad = -(-modes // 8) * 8
    half = n_rp // CORES // 2
    cos_e, sin_e = phases(kpoint_index, electron_cells)
    cos_p, sin_p = phases(qpoint_index, phonon_cells)
    vec = eigenvectors[0].reshape(2, modes, n_mode, modes)
    vec = jnp.pad(vec, ((0, 0), (0, pad - modes), (0, 0), (0, pad - modes)))
    vec = vec.transpose(0, 2, 3, 1)
    upper = jnp.concatenate([vec[0], -vec[1]], axis=-1)
    lower = jnp.concatenate([vec[1], vec[0]], axis=-1)
    turn = jnp.stack([upper, lower], axis=1).reshape(n_mode * 2 * pad, 2 * pad)

    block = (2, pad, width)
    smem = pl.BlockSpec(memory_space=pltpu.SMEM)
    vmem = pl.BlockSpec(memory_space=pltpu.VMEM)
    peers, others = max(n_re - 1, 1), max(n_mode - 1, 1)
    dma = pltpu.SemaphoreType.DMA
    rest = max(half - 1, 1)
    f32 = jnp.float32
    rotated = pl.pallas_call(
        functools.partial(kernel, (n_re, n_rp, n_mode, chunks, width)),
        out_shape=jax.ShapeDtypeStruct((k_local, 2, modes, pairs), f32),
        in_specs=[vmem, smem, smem, smem, smem, vmem],
        out_specs=vmem,
        scratch_shapes=[
            pltpu.VMEM((peers, chunks) + block, f32),
            pltpu.VMEM((peers, chunks) + block, f32),
            pltpu.VMEM((2 * half, chunks) + block, f32),
            pltpu.VMEM((rest, CORES, chunks) + block, f32),
            pltpu.VMEM((half, CORES, chunks) + block, f32),
            pltpu.VMEM((chunks,) + block, f32),
            pltpu.VMEM((chunks,) + block, f32),
            pltpu.VMEM((chunks,) + block, f32),
            pltpu.VMEM((2 * pad, width), f32),
            pltpu.VMEM((n_mode, chunks) + block, f32),
            pltpu.VMEM((others, chunks) + block, f32),
            dma((peers, chunks)), dma((peers, chunks)),
            dma((half, chunks)), dma((2 * half, chunks)),
            dma((rest, CORES, chunks)), dma((half, CORES, chunks)),
            dma((chunks,)), dma((chunks,)),
            dma((others, chunks)), dma((others, chunks)),
        ],
        compiler_params=pltpu.CompilerParams(
            collective_id=0, has_side_effects=True, vmem_limit_bytes=48 * 1024 * 1024
        ),
    )(coupling, cos_e, sin_e, cos_p, sin_p, turn)
    factor = lax.rsqrt(2.0 * frequencies).T[:, :, None, None, None]
    return rotated.transpose(2, 0, 1, 3)[:, None] * factor


def solution(mesh):
    placed = (
        P(None, "re", "rp", "mode", None),
        P(),
        P(),
        P(),
        P(),
        P("rp", None, "mode", None),
        P("rp", "mode"),
    )
    return jax.shard_map(
        shards,
        mesh=mesh,
        in_specs=placed,
        out_specs=P("mode", "rp", "re", None, None),
        check_vma=False,
    )
```

time: 236 us -> 69.4 us (0.29)
  waiting for transfers between devices: 185 us -> 0 us
  Pallas kernels: 0 us -> 62 us
  between operations: 14.6 us -> 0.09 us
  other arithmetic: 16.1 us -> 1.88 us
  matrix products: 8.36 us -> 0 us
  local copies, waits for them, and re-layouts: 10.4 us -> 5.16 us
    unnamed x6 -> x0, waiting for transfers between devices: 185 us -> none
    pallas_call x0 -> x1, Pallas kernels: none -> 62 us  [shards(): pl.pallas_call(functools.partial(kernel, (n_re, n_rp, n_mode, chunks, wid...]
    dot_general x3 -> x0, matrix products: 8.36 us -> none  [the longest x1 4.3 us: electron_apply(): jnp.dot(complex_rows(cos_t, sin_t), flat, precision=lax.Precision.HIGHEST)]
    unnamed x1 -> x0, other arithmetic: 7.82 us -> none
    another operation x10 -> x2, local copies, waits for them, and re-layouts: 5.22 us -> 1.1 us  [shards(): vec = eigenvectors[0].reshape(2, modes, n_mode, modes)]
    add x1 -> x0, other arithmetic: 3.98 us -> none  [phonon_apply(): return first_term + second_term]
    unnamed x23 -> x4, local copies, waits for them, and re-layouts: 4.88 us -> 2.74 us
  transfers between devices with their start and end apart: 3 -> 0, of which waited for: 3 -> 0; matrix products, arithmetic and copies ran while one was open for 1% -> 0% of each run, Pallas kernels for 0% -> 0%
where the time goes in v1:
time: 69.4 us; the launch traced here: 69.2 us
  Pallas kernels  62 us (89%)
  local copies, waits for them, and re-layouts  5.16 us (7%)
  other arithmetic  1.88 us (3%)
    pallas_call x1, Pallas kernels, shards(): pl.pallas_call(functools.partial(kernel, (n_re, n_rp, n_mode, chunks, wid...  62 us
    unnamed x4, local copies, waits for them, and re-layouts  2.74 us
    reduce_sum x2, other arithmetic, phases(): turns = jnp.sum(points[:, None, :] * cells[None, :, :], axis=-1) % KG  1.54 us

profile of v1, /device:TPU:0, one launch (start us, length us, event | category | flops | bytes accessed | tf_op | source)
XLA Modules:
  0.0 69.2 jit_solution(15127624560486370681)
XLA Ops:
  0.0 1.0 %reshape_squeeze.3 = f32[2,60,2,60]{3,2,0,1:T(2,128)S(1)} reshape(f32[1,2,60,120]{3,1,2,0:T(2,128)} %param.12) | data formatting | bytes 115200 | tf_op jit(solution)/shard_map/reshape;squeeze | solution.py:271
  1.0 0.1 copy.16
  1.2 0.1 maximum_bitcast_fusion
  1.3 0.8 %multiply_reduce_fusion = s32[8,8]{1,0:T(8,128)S(1)} fusion(s32[8,3]{0,1:T(4,128)} %param.9, s32[8,3]{0,1:T(4,128)} %param.11), kind=kLoop, calls=%fused_computation.7 | loop fusion | flops 320 | bytes 448 | tf_op jit(solution)/shard_map/reduce_sum | solution.py:18
  2.1 0.1 fusion.6
  2.1 0.8 %copy.15 = s32[4,3]{0,1:T(4,128)S(1)} copy(s32[4,3]{1,0:T(4,128)} %param.10) | data formatting | bytes 96 | tf_op args[3]
  2.9 0.8 %multiply_reduce_fusion.1 = s32[4,16]{1,0:T(4,128)S(1)} fusion(s32[16,3]{0,1:T(4,128)} %param.8, s32[4,3]{0,1:T(4,128)S(1)} %copy.15), kind=kLoop, calls=%fused_computation.11 | loop fusion | flops 320 | bytes 496 | tf_op jit(solution)/shard_map/reduce_sum | solution.py:18
  3.7 0.1 fusion.8
  3.7 2.0 %copy.18.coupling = f32[2,8,1,60,576]{4,3,2,1,0:T(8,128)S(1)} copy(f32[2,8,1,60,576]{4,2,3,1,0:T(1,128)} %param.7) | data formatting | bytes 4423680 | tf_op args[0]
  5.7 0.0 copy-start
  5.7 62.0 %shard_map.73 = f32[2,2,60,576]{3,2,1,0:T(8,128)S(1)} custom-call(f32[2,8,1,60,576]{4,3,2,1,0:T(8,128)S(1)} %copy.18.coupling, f32[4,16]{1,0:T(4,128)S(1)} %get-tuple-element.12.cos_e, f32[4,16]{1,0:T(4,128)S(1)} %get-tuple-element.11.sin_e, f32[8,8]{1,0:T(8,128)S(1)} %get-tuple-element.10.cos_p, f32[8,8]{1,0:T(8,128)S(1)} %get-tuple-element.9.sin_p, ...), custom_call_target="tpu_custom_call" | custom-call | tf_op jit(solution)/shard_map/pallas_call | solution.py:285
  67.7 0.0 copy-done
  67.8 0.1 multiply_bitcast_fusion
  67.9 1.3 %copy.19 = f32[60,1,2,2,576]{4,3,2,1,0:T(2,128)} copy(f32[60,1,2,2,576]{4,0,3,2,1:T(8,128)S(1)} %multiply_bitcast_fusion) | data formatting | bytes 1105920 | tf_op jit(solution)/shard_map/mul | solution.py:313
  (5 shorter events, 0.0 us)
Async XLA Ops:
  5.7 62.1 %copy-start = (f32[1,60]{1,0:T(1,128)S(1)}, f32[1,60]{1,0:T(1,128)}, u32[]{:S(2)}) copy-start(f32[1,60]{1,0:T(1,128)} %param.13) | copy-start | bytes 724

commit v2 on v1

v2 whole, which is shorter than its diff:
```python
import functools

import jax
import jax.numpy as jnp
import numpy as np
from jax import lax
from jax.experimental import pallas as pl
from jax.experimental.pallas import tpu as pltpu
from jax.sharding import PartitionSpec as P

KG = 16
CORES = 2
LANES = 128
CHUNKS = 9
MESH = pl.DeviceIdType.MESH


def segments(modes):
    base = modes // 8 * 8
    left = modes - base
    shared = 0 if left == 0 else (8 if 2 * left <= 8 else 16)
    rows = [(0, 0, base, 0), (1, 0, base, base + shared)]
    if left:
        rows += [(0, base, modes, base), (1, base, modes, base + shared // 2)]
    return base, left, shared, rows


def pieces_of(chunk, width, pairs):
    found = []
    at = chunk * width
    end = at + width
    while at < end:
        k = at // pairs
        stop = min(end, (k + 1) * pairs)
        found.append((k, at - k * pairs, stop - k * pairs, at - chunk * width))
        at = stop
    return found


def kernel(
    sizes, coupling, electron_cells, phonon_cells, kpoints, qpoints, roots, vectors, out,
    held, cos_e, sin_e, cos_p, sin_p, square, turn,
    xout, xin, raw, sumout, sumin, mine, sibout, sibin, packed, yout, yin,
    load, xs, xr, rs, rr, ss, sr, bs, br, ys, yr,
):
    n_re, n_rp, n_mode, chunks, width = sizes
    re_local, modes, pairs = coupling.shape[1], coupling.shape[3], coupling.shape[4]
    k_local = out.shape[0]
    base, left, shared, rows = segments(modes)
    tall = 2 * base + shared
    half = n_rp // CORES // 2
    me_re, me_rp, me_mode = lax.axis_index("re"), lax.axis_index("rp"), lax.axis_index("mode")
    chip, core = me_rp // CORES, me_rp % CORES
    side = jnp.where(chip >= half, 1, 0)
    depth = jnp.where(side == 1, chip - half, half - 1 - chip)

    fetch = pltpu.make_async_copy(coupling, held, load)
    fetch.start()

    def chip_at(d, s):
        return jnp.where(s == 1, half + d, half - 1 - d)

    inner = jnp.where(depth == 0, chip_at(0, 1 - side), chip_at(depth - 1, side)) * CORES + core
    outer = chip_at(jnp.minimum(depth + 1, half - 1), side) * CORES + core
    sibling = chip * CORES + 1 - core
    re_peers = [lax.rem(me_re + d, n_re) for d in range(1, n_re)]
    mode_peers = [lax.rem(me_mode + d, n_mode) for d in range(1, n_mode)]

    def remote(src, dst, send, recv, where):
        return pltpu.make_async_remote_copy(
            src_ref=src, dst_ref=dst, send_sem=send, recv_sem=recv,
            device_id=where, device_id_type=MESH,
        )

    def x_copy(d, j):
        return remote(xout.at[d, j], xin.at[d, j], xs.at[d, j], xr.at[d, j], {"re": re_peers[d]})

    def raw_copy(tt, i, j):
        to = half + i if tt == 0 else i + 1
        return remote(raw.at[i, j], raw.at[to, j], rs.at[i, j], rr.at[to, j], {"rp": inner})

    def raw_arrival(i, j):
        return remote(raw.at[i, j], raw.at[i, j], rs.at[0, j], rr.at[i, j], {"rp": inner})

    def sum_copy(i, j):
        return remote(sumout.at[i, j], sumin.at[i, j], ss.at[i, j], sr.at[i, j], {"rp": outer})

    def sum_arrival(i, j):
        return remote(sumin.at[i, j], sumin.at[i, j], ss.at[0, j], sr.at[i, j], {"rp": outer})

    def sib_copy(tt, j):
        some = pl.ds(0, half - tt)
        return remote(sibout.at[j, some], sibin.at[j, some], bs.at[j], br.at[j], {"rp": sibling})

    def y_copy(d, j):
        return remote(
            yout.at[mode_peers[d], j], yin.at[d, j], ys.at[d, j], yr.at[d, j],
            {"mode": mode_peers[d]},
        )

    barrier = pltpu.get_barrier_semaphore()

    def greet(where):
        pl.semaphore_signal(barrier, inc=1, device_id=where, device_id_type=MESH)

    for p in re_peers:
        greet({"re": p})
    for p in mode_peers:
        greet({"mode": p})
    greet({"rp": sibling})
    greet({"rp": inner})

    @pl.when(depth < half - 1)
    def _():
        greet({"rp": outer})

    def table(points, cells, first, count, cos_t, sin_t):
        for i in range(points.shape[0]):
            for s in range(count):
                turns = points[i, 0] * cells[first + s, 0]
                for axis in range(1, points.shape[1]):
                    turns = turns + points[i, axis] * cells[first + s, axis]
                cos_t[i, s] = roots[turns & (KG - 1)]
                sin_t[i, s] = roots[(turns + (KG - KG // 4)) & (KG - 1)]

    table(kpoints, electron_cells, me_re * re_local, re_local, cos_e, sin_e)

    friends = n_re - 1 + n_mode - 1 + 2
    pl.semaphore_wait(barrier, friends + jnp.where(depth < half - 1, 1, 0))
    fetch.wait()

    def electron(owner, j, dst):
        if left and 2 * left != shared:
            dst[base:base + shared, :] = jnp.zeros((shared, width), jnp.float32)
        spans = [(rows[0], rows[1])] + ([(rows[2], rows[3])] if left else [])
        for k, p0, p1, at in pieces_of(j, width, pairs):
            row = owner * k_local + k
            for (_, r0, r1, to_real), (_, _, _, to_imag) in spans:
                real = imag = None
                for r in range(re_local):
                    c, s = cos_e[row, r], sin_e[row, r]
                    a = held[0, r, 0, r0:r1, p0:p1]
                    b = held[1, r, 0, r0:r1, p0:p1]
                    x, y = c * a - s * b, c * b + s * a
                    real = x if real is None else real + x
                    imag = y if imag is None else imag + y
                dst[to_real:to_real + r1 - r0, at:at + p1 - p0] = real
                dst[to_imag:to_imag + r1 - r0, at:at + p1 - p0] = imag

    def phonon(dst, q, terms):
        factors = [(src, s_chip * CORES + core) for src, s_chip in terms]
        real = imag = both = None
        for src, s_at in factors:
            c, s = cos_p[q, s_at], sin_p[q, s_at]
            a, b = src[0:base, :], src[base + shared:tall, :]
            x, y = c * a - s * b, c * b + s * a
            real = x if real is None else real + x
            imag = y if imag is None else imag + y
        dst[0:base, :] = real
        dst[base + shared:tall, :] = imag
        if left:
            place = lax.broadcasted_iota(jnp.int32, (shared, width), 0)
            sign = jnp.where(place < shared // 2, -1.0, 1.0)
            for src, s_at in factors:
                c, s = cos_p[q, s_at], sin_p[q, s_at]
                t = src[base:base + shared, :]
                x = c * t + s * (sign * pltpu.roll(t, shared // 2, 0))
                both = x if both is None else both + x
            dst[base:base + shared, :] = both

    for j in range(chunks):
        for d in range(n_re - 1):
            electron(re_peers[d], j, xout.at[d, j])
            x_copy(d, j).start()

    table(qpoints, phonon_cells, 0, n_rp, cos_p, sin_p)

    def x_stage(j):
        electron(me_re, j, raw.at[0, j])
        for d in range(n_re - 1):
            x_copy(d, j).wait_recv()
        total = raw[0, j]
        for d in range(n_re - 1):
            total = total + xin[d, j]
        raw[0, j] = total
        for tt in range(half):
            @pl.when(depth == tt)
            def _():
                raw_copy(tt, 0, j).start()

    def forward_stage(j):
        for tt in range(half - 1):
            @pl.when(depth == tt)
            def _():
                for i in range(1, half - tt):
                    raw_arrival(i, j).wait_recv()
                    raw_copy(tt, i, j).start()

    def turn_stage():
        square[...] = jnp.zeros_like(square)
        n_all = vectors.shape[3]
        flipped = []
        for part in range(2):
            square[0:modes, 0:n_all] = vectors[0, part]
            flipped.append(jnp.transpose(square[...]))
        for m in range(n_mode):
            turn[m] = jnp.zeros(turn.shape[1:], jnp.float32)
            for to, n0, n1, at_n in rows:
                for come, c0, c1, at_c in rows:
                    block = flipped[0 if to == come else 1]
                    block = block[m * modes + n0:m * modes + n1, c0:c1]
                    if to < come:
                        block = -block
                    turn[m, at_n:at_n + n1 - n0, at_c:at_c + c1 - c0] = block

    def z_stage(j):
        for tt in range(half):
            @pl.when(depth == tt)
            def _():
                own = (raw.at[0, j], chip)
                outside = [(raw.at[i, j], chip_at(tt + i, side)) for i in range(1, half - tt)]
                across = []
                if tt == 0:
                    for i in range(half):
                        raw_arrival(half + i, j).wait_recv()
                    across = [(raw.at[half + i, j], chip_at(i, 1 - side)) for i in range(half)]
                for dst, c in ((sibout, 1 - core), (mine, core)):
                    for i in range(half - tt):
                        q = chip_at(tt + i, side) * CORES + c
                        phonon(dst.at[j, i], q, [own] + across + (outside if i == 0 else []))
                    if dst is sibout:
                        sib_copy(tt, j).start()

    def sum_stage(j):
        for tt in range(half):
            @pl.when(depth == tt)
            def _():
                sib_copy(tt, j).wait_recv()
                if tt > 0:
                    for i in range(half - tt):
                        sum_arrival(i, j).wait_recv()
                for i in list(range(1, half - tt)) + [0]:
                    total = mine[j, i] + sibin[j, i]
                    if tt > 0:
                        total = total + sumin[i, j]
                    if i == 0:
                        packed[j] = total
                    else:
                        sumout[i - 1, j] = total
                        sum_copy(i - 1, j).start()

    def mode_stage(j):
        for m in range(n_mode):
            yout[m, j] = jnp.dot(
                turn[m], packed[j], precision=lax.Precision.HIGHEST,
                preferred_element_type=jnp.float32,
            )
        for d in range(n_mode - 1):
            y_copy(d, j).start()

    def out_stage(j):
        for d in range(n_mode - 1):
            y_copy(d, j).wait_recv()
        total = yout[me_mode, j]
        for d in range(n_mode - 1):
            total = total + yin[d, j]
        for k, p0, p1, at in pieces_of(j, width, pairs):
            for part, n0, n1, at_n in rows:
                out[k, part, n0:n1, p0:p1] = total[at_n:at_n + n1 - n0, at:at + p1 - p0]

    xs_done = forwarded = 0
    turn_ready = False
    for j in range(chunks + 3):
        until = min(2 * j + 5, chunks)
        while xs_done < until:
            x_stage(xs_done)
            xs_done += 1
            while forwarded < xs_done - 1:
                forward_stage(forwarded)
                forwarded += 1
        if xs_done == chunks and forwarded < chunks:
            forward_stage(forwarded)
            forwarded += 1
        if not turn_ready:
            turn_stage()
            turn_ready = True
        if j < chunks:
            z_stage(j)
        if 1 <= j <= chunks:
            sum_stage(j - 1)
            mode_stage(j - 1)
        if 3 <= j:
            out_stage(j - 3)

    for j in range(chunks):
        for d in range(n_re - 1):
            x_copy(d, j).wait_send()
        for d in range(n_mode - 1):
            y_copy(d, j).wait_send()
        for tt in range(half):
            @pl.when(depth == tt)
            def _():
                sib_copy(tt, j).wait_send()
                for i in range(half - tt):
                    raw_copy(tt, i, j).wait_send()
                for i in range(half - 1 - tt):
                    sum_copy(i, j).wait_send()


def shards(
    coupling, electron_cells, phonon_cells, kpoint_index, qpoint_index, eigenvectors, frequencies
):
    n_re, n_rp, n_mode = lax.axis_size("re"), lax.axis_size("rp"), lax.axis_size("mode")
    modes, pairs = coupling.shape[3], coupling.shape[4]
    k_all, q_all = kpoint_index.shape[0], qpoint_index.shape[0]
    k_local = k_all // n_re
    columns = k_local * pairs
    chunks = CHUNKS if columns % (CHUNKS * LANES) == 0 else 1
    width = columns // chunks
    base, _, shared, _ = segments(modes)
    tall = 2 * base + shared
    half = n_rp // CORES // 2
    side = -(-eigenvectors.shape[3] // LANES) * LANES
    roots = jnp.asarray(np.cos(np.arange(KG) * (2.0 * np.pi / KG)).astype(np.float32))

    block = (tall, width)
    smem = pl.BlockSpec(memory_space=pltpu.SMEM)
    vmem = pl.BlockSpec(memory_space=pltpu.VMEM)
    peers, others = max(n_re - 1, 1), max(n_mode - 1, 1)
    dma = pltpu.SemaphoreType.DMA
    rest = max(half - 1, 1)
    f32 = jnp.float32
    rotated = pl.pallas_call(
        functools.partial(kernel, (n_re, n_rp, n_mode, chunks, width)),
        out_shape=jax.ShapeDtypeStruct((k_local, 2, modes, pairs), f32),
        in_specs=[pl.BlockSpec(memory_space=pl.ANY)] + [smem] * 5 + [vmem],
        out_specs=vmem,
        scratch_shapes=[
            pltpu.VMEM(coupling.shape, f32),
            pltpu.SMEM((k_all, coupling.shape[1]), f32),
            pltpu.SMEM((k_all, coupling.shape[1]), f32),
            pltpu.SMEM((q_all, n_rp), f32),
            pltpu.SMEM((q_all, n_rp), f32),
            pltpu.VMEM((side, side), f32),
            pltpu.VMEM((n_mode, tall, tall), f32),
            pltpu.VMEM((peers, chunks) + block, f32),
            pltpu.VMEM((peers, chunks) + block, f32),
            pltpu.VMEM((2 * half, chunks) + block, f32),
            pltpu.VMEM((rest, chunks) + block, f32),
            pltpu.VMEM((half, chunks) + block, f32),
            pltpu.VMEM((chunks, half) + block, f32),
            pltpu.VMEM((chunks, half) + block, f32),
            pltpu.VMEM((chunks, half) + block, f32),
            pltpu.VMEM((chunks,) + block, f32),
            pltpu.VMEM((n_mode, chunks) + block, f32),
            pltpu.VMEM((others, chunks) + block, f32),
            dma, dma((peers, chunks)), dma((peers, chunks)),
            dma((half, chunks)), dma((2 * half, chunks)),
            dma((rest, chunks)), dma((half, chunks)),
            dma((chunks,)), dma((chunks,)),
            dma((others, chunks)), dma((others, chunks)),
        ],
        compiler_params=pltpu.CompilerParams(
            collective_id=0, has_side_effects=True, vmem_limit_bytes=56 * 1024 * 1024
        ),
    )(coupling, electron_cells, phonon_cells, kpoint_index, qpoint_index, roots, eigenvectors)
    factor = lax.rsqrt(2.0 * frequencies).T[:, :, None, None, None]
    return rotated.transpose(2, 0, 1, 3)[:, None] * factor


def solution(mesh):
    placed = (
        P(None, "re", "rp", "mode", None),
        P(),
        P(),
        P(),
        P(),
        P("rp", None, "mode", None),
        P("rp", "mode"),
    )
    return jax.shard_map(
        shards,
        mesh=mesh,
        in_specs=placed,
        out_specs=P("mode", "rp", "re", None, None),
        check_vma=False,
    )
```

time: 69.4 us -> 56.2 us (0.81)
  Pallas kernels: 62 us -> 47.3 us
  local copies, waits for them, and re-layouts: 5.16 us -> 7.43 us
    pallas_call x1, Pallas kernels: 62 us -> 47.3 us  [shards(): pl.pallas_call(functools.partial(kernel, (n_re, n_rp, n_mode, chunks, wid...]
    unnamed x4 -> x15, local copies, waits for them, and re-layouts: 2.74 us -> 6.13 us
    reduce_sum x2 -> x0, other arithmetic: 1.54 us -> none  [phases(): turns = jnp.sum(points[:, None, :] * cells[None, :, :], axis=-1) % KG]
    another operation x2 -> x0, local copies, waits for them, and re-layouts: 1.1 us -> none  [shards(): vec = eigenvectors[0].reshape(2, modes, n_mode, modes)]
    mul x2, other arithmetic: 0.12 us -> 1.2 us  [shards(): return rotated.transpose(2, 0, 1, 3)[:, None] * factor]
where the time goes in v2:
time: 56.2 us; the launch traced here: 56 us
  Pallas kernels  47.3 us (84%)
  local copies, waits for them, and re-layouts  7.43 us (13%)
  other arithmetic  1.2 us (2%)
    pallas_call x1, Pallas kernels, shards(): pl.pallas_call(functools.partial(kernel, (n_re, n_rp, n_mode, chunks, wid...  47.3 us
    unnamed x15, local copies, waits for them, and re-layouts  6.13 us
    mul x1, local copies, waits for them, and re-layouts, shards(): return rotated.transpose(2, 0, 1, 3)[:, None] * factor  1.3 us
    mul x2, other arithmetic, shards(): return rotated.transpose(2, 0, 1, 3)[:, None] * factor  1.2 us

profile of v2, /device:TPU:0, one launch (start us, length us, event | category | flops | bytes accessed | tf_op | source)
XLA Modules:
  0.0 56.0 jit_solution(17135079726832957380)
XLA Ops:
  0.0 0.0 copy-start
  0.0 0.0 copy-start.1
  0.0 0.0 copy-start.2
  0.0 0.0 copy-start.3
  0.0 3.5 %copy.9.coupling = f32[2,8,1,60,576]{4,3,2,1,0:T(8,128)} copy(f32[2,8,1,60,576]{4,2,3,1,0:T(1,128)} %param.8) | data formatting | bytes 4423680 | tf_op args[0]
  3.5 0.0 copy-done
  3.5 0.0 copy-start.4
  3.5 0.6 %copy.13.vectors = f32[1,2,60,120]{3,2,1,0:T(8,128)} copy(f32[1,2,60,120]{3,1,2,0:T(2,128)S(1)} %copy-done) | data formatting | bytes 115200 | tf_op args[5]
  4.1 0.0 copy-done.1
  4.1 0.7 %copy.10.electron_cells = s32[16,3]{1,0:T(8,128)} copy(s32[16,3]{0,1:T(4,128)S(1)} %copy-done.1) | data formatting | bytes 384 | tf_op args[1]
  4.8 0.0 copy-done.2
  4.8 0.7 %copy.11.phonon_cells = s32[8,3]{1,0:T(8,128)} copy(s32[8,3]{0,1:T(4,128)S(1)} %copy-done.2) | data formatting | bytes 192 | tf_op args[2]
  5.5 0.0 copy-done.3
  5.5 0.7 %copy.12.qpoints = s32[8,3]{1,0:T(8,128)} copy(s32[8,3]{0,1:T(4,128)S(1)} %copy-done.3) | data formatting | bytes 192 | tf_op args[4]
  6.1 47.3 %shard_map.82 = f32[2,2,60,576]{3,2,1,0:T(8,128)} custom-call(f32[2,8,1,60,576]{4,3,2,1,0:T(8,128)} %copy.9.coupling, s32[16,3]{1,0:T(8,128)} %copy.10.electron_cells, s32[8,3]{1,0:T(8,128)} %copy.11.phonon_cells, s32[4,3]{1,0:T(4,128)} %kpoints.1, s32[8,3]{1,0:T(8,128)} %copy.12.qpoints, f32[16]{0:T(128)} %constant.4.clone.roots, ...), custom_call_target="tpu_custom_call" | custom-call | tf_op jit(solution)/shard_map/pallas_call | solution.py:333
  53.5 0.0 copy-done.4
  53.5 1.2 %multiply_bitcast_fusion = f32[60,1,2,2,576]{4,0,3,2,1:T(8,128)S(1)} fusion(f32[2,2,60,576]{3,2,1,0:T(8,128)} %shard_map.82, f32[60]{0:T(128)S(1)} %rsqrt_bitcast_fusion), kind=kLoop, calls=%fused_computation | loop fusion | flops 138240 | bytes 1106160 | tf_op jit(solution)/shard_map/mul | solution.py:368
  54.7 1.3 %copy.14 = f32[60,1,2,2,576]{4,3,2,1,0:T(2,128)} copy(f32[60,1,2,2,576]{4,0,3,2,1:T(8,128)S(1)} %multiply_bitcast_fusion) | data formatting | bytes 1105920 | tf_op jit(solution)/shard_map/mul | solution.py:368
  (1 shorter events, 0.0 us)
Async XLA Ops:
  0.0 3.5 %copy-start = (f32[1,2,60,120]{3,1,2,0:T(2,128)S(1)}, f32[1,2,60,120]{3,1,2,0:T(2,128)}, u32[]{:S(2)}) copy-start(f32[1,2,60,120]{3,1,2,0:T(2,128)} %param.13) | copy-start | bytes 172804
  0.0 4.1 %copy-start.1 = (s32[16,3]{0,1:T(4,128)S(1)}, s32[16,3]{0,1:T(4,128)}, u32[]{:S(2)}) copy-start(s32[16,3]{0,1:T(4,128)} %param.9) | copy-start | bytes 580
  0.0 4.8 %copy-start.2 = (s32[8,3]{0,1:T(4,128)S(1)}, s32[8,3]{0,1:T(4,128)}, u32[]{:S(2)}) copy-start(s32[8,3]{0,1:T(4,128)} %param.10) | copy-start | bytes 292
  0.0 5.5 %copy-start.3 = (s32[8,3]{0,1:T(4,128)S(1)}, s32[8,3]{0,1:T(4,128)}, u32[]{:S(2)}) copy-start(s32[8,3]{0,1:T(4,128)} %param.12) | copy-start | bytes 292
  3.5 50.0 %copy-start.4 = (f32[1,60]{1,0:T(1,128)S(1)}, f32[1,60]{1,0:T(1,128)}, u32[]{:S(2)}) copy-start(f32[1,60]{1,0:T(1,128)} %param.14) | copy-start | bytes 724

commit v3 on v2

--- a/solution.py
+++ b/solution.py
@@ -12,6 +12,7 @@
 CORES = 2
 LANES = 128
 CHUNKS = 9
+LEAD = 4
 MESH = pl.DeviceIdType.MESH
 
 
@@ -23,6 +24,11 @@
     if left:
         rows += [(0, base, modes, base), (1, base, modes, base + shared // 2)]
     return base, left, shared, rows
+
+
+def split(x):
+    high = x.astype(jnp.bfloat16)
+    return high, (x - high.astype(jnp.float32)).astype(jnp.bfloat16)
 
 
 def pieces_of(chunk, width, pairs):
@@ -44,7 +50,7 @@
     load, xs, xr, rs, rr, ss, sr, bs, br, ys, yr,
 ):
     n_re, n_rp, n_mode, chunks, width = sizes
-    re_local, modes, pairs = coupling.shape[1], coupling.shape[3], coupling.shape[4]
+    re_local, modes, pairs = coupling.shape[1], coupling.shape[2], coupling.shape[4]
     k_local = out.shape[0]
     base, left, shared, rows = segments(modes)
     tall = 2 * base + shared
@@ -54,7 +60,7 @@
     side = jnp.where(chip >= half, 1, 0)
     depth = jnp.where(side == 1, chip - half, half - 1 - chip)
 
-    fetch = pltpu.make_async_copy(coupling, held, load)
+    fetch = pltpu.make_async_copy(coupling.at[:, :, :, 0, :], held, load)
     fetch.start()
 
     def chip_at(d, s):
@@ -114,16 +120,16 @@
     def _():
         greet({"rp": outer})
 
-    def table(points, cells, first, count, cos_t, sin_t):
-        for i in range(points.shape[0]):
+    def table(points, point, cells, first, count, cos_t, sin_t):
+        for i in range(points):
             for s in range(count):
-                turns = points[i, 0] * cells[first + s, 0]
-                for axis in range(1, points.shape[1]):
-                    turns = turns + points[i, axis] * cells[first + s, axis]
+                turns = point(i, 0) * cells[0, first + s]
+                for axis in range(1, cells.shape[0]):
+                    turns = turns + point(i, axis) * cells[axis, first + s]
                 cos_t[i, s] = roots[turns & (KG - 1)]
                 sin_t[i, s] = roots[(turns + (KG - KG // 4)) & (KG - 1)]
 
-    table(kpoints, electron_cells, me_re * re_local, re_local, cos_e, sin_e)
+    table(cos_e.shape[0], lambda i, a: kpoints[i, a], electron_cells, me_re * re_local, re_local, cos_e, sin_e)
 
     friends = n_re - 1 + n_mode - 1 + 2
     pl.semaphore_wait(barrier, friends + jnp.where(depth < half - 1, 1, 0))
@@ -139,8 +145,8 @@
                 real = imag = None
                 for r in range(re_local):
                     c, s = cos_e[row, r], sin_e[row, r]
-                    a = held[0, r, 0, r0:r1, p0:p1]
-                    b = held[1, r, 0, r0:r1, p0:p1]
+                    a = held[0, r, r0:r1, p0:p1]
+                    b = held[1, r, r0:r1, p0:p1]
                     x, y = c * a - s * b, c * b + s * a
                     real = x if real is None else real + x
                     imag = y if imag is None else imag + y
@@ -168,12 +174,15 @@
                 both = x if both is None else both + x
             dst[base:base + shared, :] = both
 
-    for j in range(chunks):
+    def peer_stage(j):
         for d in range(n_re - 1):
             electron(re_peers[d], j, xout.at[d, j])
             x_copy(d, j).start()
 
-    table(qpoints, phonon_cells, 0, n_rp, cos_p, sin_p)
+    for j in range(min(LEAD, chunks)):
+        peer_stage(j)
+
+    table(cos_p.shape[0], lambda i, a: qpoints[a, i], phonon_cells, 0, n_rp, cos_p, sin_p)
 
     def x_stage(j):
         electron(me_re, j, raw.at[0, j])
@@ -187,6 +196,8 @@
             @pl.when(depth == tt)
             def _():
                 raw_copy(tt, 0, j).start()
+        if j + LEAD < chunks:
+            peer_stage(j + LEAD)
 
     def forward_stage(j):
         for tt in range(half - 1):
@@ -201,7 +212,7 @@
         n_all = vectors.shape[3]
         flipped = []
         for part in range(2):
-            square[0:modes, 0:n_all] = vectors[0, part]
+            square[0:modes, 0:n_all] = vectors[0, :, part, :]
             flipped.append(jnp.transpose(square[...]))
         for m in range(n_mode):
             turn[m] = jnp.zeros(turn.shape[1:], jnp.float32)
@@ -250,11 +261,14 @@
                         sum_copy(i - 1, j).start()
 
     def mode_stage(j):
-        for m in range(n_mode):
-            yout[m, j] = jnp.dot(
-                turn[m], packed[j], precision=lax.Precision.HIGHEST,
-                preferred_element_type=jnp.float32,
-            )
+        w_high, w_low = split(turn[...].reshape(n_mode * tall, tall))
+        x_high, x_low = split(packed[j])
+
+        def product(w, x):
+            return jnp.dot(w, x, preferred_element_type=jnp.float32)
+
+        turned = product(w_high, x_low) + product(w_low, x_high) + product(w_high, x_high)
+        yout[:, j] = turned.reshape(n_mode, tall, width)
         for d in range(n_mode - 1):
             y_copy(d, j).start()
 
@@ -271,7 +285,7 @@
     xs_done = forwarded = 0
     turn_ready = False
     for j in range(chunks + 3):
-        until = min(2 * j + 5, chunks)
+        until = min(3 * j + 6, chunks)
         while xs_done < until:
             x_stage(xs_done)
             xs_done += 1
@@ -336,7 +350,7 @@
         in_specs=[pl.BlockSpec(memory_space=pl.ANY)] + [smem] * 5 + [vmem],
         out_specs=vmem,
         scratch_shapes=[
-            pltpu.VMEM(coupling.shape, f32),
+            pltpu.VMEM((2, coupling.shape[1], modes, pairs), f32),
             pltpu.SMEM((k_all, coupling.shape[1]), f32),
             pltpu.SMEM((k_all, coupling.shape[1]), f32),
             pltpu.SMEM((q_all, n_rp), f32),
@@ -363,7 +377,10 @@
         compiler_params=pltpu.CompilerParams(
             collective_id=0, has_side_effects=True, vmem_limit_bytes=56 * 1024 * 1024
         ),
-    )(coupling, electron_cells, phonon_cells, kpoint_index, qpoint_index, roots, eigenvectors)
+    )(
+        coupling.transpose(0, 1, 3, 2, 4), electron_cells.T, phonon_cells.T, kpoint_index,
+        qpoint_index.T, roots, eigenvectors.transpose(0, 2, 1, 3),
+    )
     factor = lax.rsqrt(2.0 * frequencies).T[:, :, None, None, None]
     return rotated.transpose(2, 0, 1, 3)[:, None] * factor
 

time: 56.2 us -> 49.7 us (0.88)
  local copies, waits for them, and re-layouts: 7.43 us -> 1.3 us
  Pallas kernels: 47.3 us -> 46.4 us
  other arithmetic: 1.2 us -> 1.86 us
    unnamed x15 -> x0, local copies, waits for them, and re-layouts: 6.13 us -> none
    pallas_call x1, Pallas kernels: 47.3 us -> 46.4 us  [shards(): pl.pallas_call(functools.partial(kernel, (n_re, n_rp, n_mode, chunks, wid...]
    mul x2, other arithmetic: 1.2 us -> 1.86 us  [shards(): return rotated.transpose(2, 0, 1, 3)[:, None] * factor]
where the time goes in v3:
time: 49.7 us; the launch traced here: 49.5 us
  Pallas kernels  46.4 us (93%)
  other arithmetic  1.86 us (4%)
  local copies, waits for them, and re-layouts  1.3 us (3%)
    pallas_call x1, Pallas kernels, shards(): pl.pallas_call(functools.partial(kernel, (n_re, n_rp, n_mode, chunks, wid...  46.4 us
    mul x2, other arithmetic, shards(): return rotated.transpose(2, 0, 1, 3)[:, None] * factor  1.86 us
    mul x1, local copies, waits for them, and re-layouts, shards(): return rotated.transpose(2, 0, 1, 3)[:, None] * factor  1.3 us

profile of v3, /device:TPU:0, one launch (start us, length us, event | category | flops | bytes accessed | tf_op | source)
XLA Modules:
  0.0 49.5 jit_solution(4056083234497990516)
XLA Ops:
  0.0 0.7 %rsqrt_bitcast_fusion = f32[60]{0:T(128)S(1)} fusion(f32[1,60]{1,0:T(1,128)} %param.14), kind=kLoop, calls=%fused_computation.1 | loop fusion | flops 60 | bytes 480 | tf_op jit(solution)/shard_map/mul | solution.py:385
  0.7 46.4 %shard_map.82 = f32[2,2,60,576]{3,2,1,0:T(8,128)} custom-call(f32[2,8,60,1,576]{4,3,2,1,0:T(1,128)} %bitcast.11, s32[3,16]{1,0:T(4,128)} %bitcast.13, s32[3,8]{1,0:T(4,128)} %bitcast.14, s32[4,3]{1,0:T(4,128)} %kpoints.1, s32[3,8]{1,0:T(4,128)} %bitcast.15, f32[16]{0:T(128)} %constant.4.clone.roots, f32[1,60,2,120]{3,2,1,0:T(2,128)} %bitcast.12), custom_call_target="tpu_custom_call" | custom-call | tf_op jit(solution)/shard_map/pallas_call | solution.py:347
  47.0 1.2 %multiply_bitcast_fusion = f32[60,1,2,2,576]{4,0,3,2,1:T(8,128)S(1)} fusion(f32[2,2,60,576]{3,2,1,0:T(8,128)} %shard_map.82, f32[60]{0:T(128)S(1)} %rsqrt_bitcast_fusion), kind=kLoop, calls=%fused_computation | loop fusion | flops 138240 | bytes 1106160 | tf_op jit(solution)/shard_map/mul | solution.py:385
  48.2 1.3 %copy.9 = f32[60,1,2,2,576]{4,3,2,1,0:T(2,128)} copy(f32[60,1,2,2,576]{4,0,3,2,1:T(8,128)S(1)} %multiply_bitcast_fusion) | data formatting | bytes 1105920 | tf_op jit(solution)/shard_map/mul | solution.py:385

commit v4 on v3

--- a/solution.py
+++ b/solution.py
@@ -51,7 +51,7 @@
 ):
     n_re, n_rp, n_mode, chunks, width = sizes
     re_local, modes, pairs = coupling.shape[1], coupling.shape[2], coupling.shape[4]
-    k_local = out.shape[0]
+    k_local = out.shape[1]
     base, left, shared, rows = segments(modes)
     tall = 2 * base + shared
     half = n_rp // CORES // 2
@@ -60,8 +60,15 @@
     side = jnp.where(chip >= half, 1, 0)
     depth = jnp.where(side == 1, chip - half, half - 1 - chip)
 
-    fetch = pltpu.make_async_copy(coupling.at[:, :, :, 0, :], held, load)
-    fetch.start()
+    fetches = []
+    for p in range(0, pairs, LANES):
+        span = pl.ds(p, min(LANES, pairs - p))
+        fetches.append(pltpu.make_async_copy(
+            coupling.at[:, :, :, 0, span], held.at[:, :, :, span], load.at[len(fetches)]
+        ))
+    for fetch in fetches:
+        fetch.start()
+    fetched = []
 
     def chip_at(d, s):
         return jnp.where(s == 1, half + d, half - 1 - d)
@@ -133,7 +140,6 @@
 
     friends = n_re - 1 + n_mode - 1 + 2
     pl.semaphore_wait(barrier, friends + jnp.where(depth < half - 1, 1, 0))
-    fetch.wait()
 
     def electron(owner, j, dst):
         if left and 2 * left != shared:
@@ -141,6 +147,9 @@
         spans = [(rows[0], rows[1])] + ([(rows[2], rows[3])] if left else [])
         for k, p0, p1, at in pieces_of(j, width, pairs):
             row = owner * k_local + k
+            while len(fetched) * LANES < p1:
+                fetches[len(fetched)].wait()
+                fetched.append(p1)
             for (_, r0, r1, to_real), (_, _, _, to_imag) in spans:
                 real = imag = None
                 for r in range(re_local):
@@ -280,7 +289,7 @@
             total = total + yin[d, j]
         for k, p0, p1, at in pieces_of(j, width, pairs):
             for part, n0, n1, at_n in rows:
-                out[k, part, n0:n1, p0:p1] = total[at_n:at_n + n1 - n0, at:at + p1 - p0]
+                out[n0:n1, k, part, p0:p1] = total[at_n:at_n + n1 - n0, at:at + p1 - p0]
 
     xs_done = forwarded = 0
     turn_ready = False
@@ -346,7 +355,7 @@
     f32 = jnp.float32
     rotated = pl.pallas_call(
         functools.partial(kernel, (n_re, n_rp, n_mode, chunks, width)),
-        out_shape=jax.ShapeDtypeStruct((k_local, 2, modes, pairs), f32),
+        out_shape=jax.ShapeDtypeStruct((modes, k_local, 2, pairs), f32),
         in_specs=[pl.BlockSpec(memory_space=pl.ANY)] + [smem] * 5 + [vmem],
         out_specs=vmem,
         scratch_shapes=[
@@ -368,7 +377,7 @@
             pltpu.VMEM((chunks,) + block, f32),
             pltpu.VMEM((n_mode, chunks) + block, f32),
             pltpu.VMEM((others, chunks) + block, f32),
-            dma, dma((peers, chunks)), dma((peers, chunks)),
+            dma((-(-pairs // LANES),)), dma((peers, chunks)), dma((peers, chunks)),
             dma((half, chunks)), dma((2 * half, chunks)),
             dma((rest, chunks)), dma((half, chunks)),
             dma((chunks,)), dma((chunks,)),
@@ -382,7 +391,7 @@
         qpoint_index.T, roots, eigenvectors.transpose(0, 2, 1, 3),
     )
     factor = lax.rsqrt(2.0 * frequencies).T[:, :, None, None, None]
-    return rotated.transpose(2, 0, 1, 3)[:, None] * factor
+    return rotated[:, None] * factor
 
 
 def solution(mesh):

time: 49.7 us -> 49.4 us (level)
  local copies, waits for them, and re-layouts: 1.3 us -> 0 us
  other arithmetic: 1.86 us -> 2.83 us
    mul x1 -> x0, local copies, waits for them, and re-layouts: 1.3 us -> none  [shards(): return rotated.transpose(2, 0, 1, 3)[:, None] * factor]
    mul x2, other arithmetic: 1.86 us -> 2.83 us  [shards(): return rotated[:, None] * factor]
where the time goes in v4:
time: 49.4 us; the launch traced here: 49.2 us
  Pallas kernels  46.3 us (94%)
  other arithmetic  2.83 us (6%)
    pallas_call x1, Pallas kernels, shards(): pl.pallas_call(functools.partial(kernel, (n_re, n_rp, n_mode, chunks, wid...  46.3 us
    mul x2, other arithmetic, shards(): return rotated[:, None] * factor  2.83 us

profile of v4, /device:TPU:0, one launch (start us, length us, event | category | flops | bytes accessed | tf_op | source)
XLA Modules:
  0.0 49.2 jit_solution(7249172383405837119)
XLA Ops:
  0.0 0.7 %rsqrt_bitcast_fusion = f32[60]{0:T(128)S(1)} fusion(f32[1,60]{1,0:T(1,128)} %param.14), kind=kLoop, calls=%fused_computation.1 | loop fusion | flops 60 | bytes 480 | tf_op jit(solution)/shard_map/mul | solution.py:394
  0.7 46.3 %shard_map.82 = f32[60,2,2,576]{3,2,1,0:T(2,128)} custom-call(f32[2,8,60,1,576]{4,3,2,1,0:T(1,128)} %bitcast.11, s32[3,16]{1,0:T(4,128)} %bitcast.13, s32[3,8]{1,0:T(4,128)} %bitcast.14, s32[4,3]{1,0:T(4,128)} %kpoints.1, s32[3,8]{1,0:T(4,128)} %bitcast.15, f32[16]{0:T(128)} %constant.4.clone.roots, f32[1,60,2,120]{3,2,1,0:T(2,128)} %bitcast.12), custom_call_target="tpu_custom_call" | custom-call | tf_op jit(solution)/shard_map/pallas_call | solution.py:356
  47.0 2.2 %multiply_bitcast_fusion = f32[60,1,2,2,576]{4,3,2,1,0:T(2,128)} fusion(f32[60,2,2,576]{3,2,1,0:T(2,128)} %shard_map.82, f32[60]{0:T(128)S(1)} %rsqrt_bitcast_fusion), kind=kLoop, calls=%fused_computation | loop fusion | flops 138240 | bytes 1106160 | tf_op jit(solution)/shard_map/mul | solution.py:394

commit v5 on v4

--- a/solution.py
+++ b/solution.py
@@ -13,6 +13,7 @@
 LANES = 128
 CHUNKS = 9
 LEAD = 4
+FLIGHT = 2
 MESH = pl.DeviceIdType.MESH
 
 
@@ -204,6 +205,8 @@
         for tt in range(half):
             @pl.when(depth == tt)
             def _():
+                if tt == 0 and j >= FLIGHT:
+                    raw_copy(tt, 0, j - FLIGHT).wait_send()
                 raw_copy(tt, 0, j).start()
         if j + LEAD < chunks:
             peer_stage(j + LEAD)
@@ -214,6 +217,8 @@
             def _():
                 for i in range(1, half - tt):
                     raw_arrival(i, j).wait_recv()
+                    if tt == 0 and j >= FLIGHT:
+                        raw_copy(tt, i, j - FLIGHT).wait_send()
                     raw_copy(tt, i, j).start()
 
     def turn_stage():
@@ -294,7 +299,7 @@
     xs_done = forwarded = 0
     turn_ready = False
     for j in range(chunks + 3):
-        until = min(3 * j + 6, chunks)
+        until = min(j + 5, chunks)
         while xs_done < until:
             x_stage(xs_done)
             xs_done += 1
@@ -325,7 +330,8 @@
             def _():
                 sib_copy(tt, j).wait_send()
                 for i in range(half - tt):
-                    raw_copy(tt, i, j).wait_send()
+                    if tt > 0 or j + FLIGHT >= chunks:
+                        raw_copy(tt, i, j).wait_send()
                 for i in range(half - 1 - tt):
                     sum_copy(i, j).wait_send()
 

time: 49.4 us -> 54.4 us (1.10)
  Pallas kernels: 46.3 us -> 51.3 us
    pallas_call x1, Pallas kernels: 46.3 us -> 51.3 us  [shards(): pl.pallas_call(functools.partial(kernel, (n_re, n_rp, n_mode, chunks, wid...]
where the time goes in v5:
time: 54.4 us; the launch traced here: 54.2 us
  Pallas kernels  51.3 us (94%)
  other arithmetic  2.83 us (5%)
    pallas_call x1, Pallas kernels, shards(): pl.pallas_call(functools.partial(kernel, (n_re, n_rp, n_mode, chunks, wid...  51.3 us
    mul x2, other arithmetic, shards(): return rotated[:, None] * factor  2.83 us

profile of v5, /device:TPU:0, one launch (start us, length us, event | category | flops | bytes accessed | tf_op | source)
XLA Modules:
  0.0 54.2 jit_solution(11097638931885335111)
XLA Ops:
  0.0 0.7 %rsqrt_bitcast_fusion = f32[60]{0:T(128)S(1)} fusion(f32[1,60]{1,0:T(1,128)} %param.14), kind=kLoop, calls=%fused_computation.1 | loop fusion | flops 60 | bytes 480 | tf_op jit(solution)/shard_map/mul | solution.py:400
  0.7 51.3 %shard_map.82 = f32[60,2,2,576]{3,2,1,0:T(2,128)} custom-call(f32[2,8,60,1,576]{4,3,2,1,0:T(1,128)} %bitcast.11, s32[3,16]{1,0:T(4,128)} %bitcast.13, s32[3,8]{1,0:T(4,128)} %bitcast.14, s32[4,3]{1,0:T(4,128)} %kpoints.1, s32[3,8]{1,0:T(4,128)} %bitcast.15, f32[16]{0:T(128)} %constant.4.clone.roots, f32[1,60,2,120]{3,2,1,0:T(2,128)} %bitcast.12), custom_call_target="tpu_custom_call" | custom-call | tf_op jit(solution)/shard_map/pallas_call | solution.py:362
  52.0 2.2 %multiply_bitcast_fusion = f32[60,1,2,2,576]{4,3,2,1,0:T(2,128)} fusion(f32[60,2,2,576]{3,2,1,0:T(2,128)} %shard_map.82, f32[60]{0:T(128)S(1)} %rsqrt_bitcast_fusion), kind=kLoop, calls=%fused_computation | loop fusion | flops 138240 | bytes 1106160 | tf_op jit(solution)/shard_map/mul | solution.py:400

commit v6 on v4

--- a/solution.py
+++ b/solution.py
@@ -294,7 +294,7 @@
     xs_done = forwarded = 0
     turn_ready = False
     for j in range(chunks + 3):
-        until = min(3 * j + 6, chunks)
+        until = chunks
         while xs_done < until:
             x_stage(xs_done)
             xs_done += 1

time: 49.4 us -> 49.4 us (level)
  no operation moved by 1% of the time
where the time goes in v6:
time: 49.4 us; the launch traced here: 49.2 us
  Pallas kernels  46.3 us (94%)
  other arithmetic  2.83 us (6%)
    pallas_call x1, Pallas kernels, shards(): pl.pallas_call(functools.partial(kernel, (n_re, n_rp, n_mode, chunks, wid...  46.3 us
    mul x2, other arithmetic, shards(): return rotated[:, None] * factor  2.83 us

profile of v6, /device:TPU:0, one launch (start us, length us, event | category | flops | bytes accessed | tf_op | source)
XLA Modules:
  0.0 49.2 jit_solution(17890151978187964545)
XLA Ops:
  0.0 0.7 %rsqrt_bitcast_fusion = f32[60]{0:T(128)S(1)} fusion(f32[1,60]{1,0:T(1,128)} %param.14), kind=kLoop, calls=%fused_computation.1 | loop fusion | flops 60 | bytes 480 | tf_op jit(solution)/shard_map/mul | solution.py:394
  0.7 46.3 %shard_map.82 = f32[60,2,2,576]{3,2,1,0:T(2,128)} custom-call(f32[2,8,60,1,576]{4,3,2,1,0:T(1,128)} %bitcast.11, s32[3,16]{1,0:T(4,128)} %bitcast.13, s32[3,8]{1,0:T(4,128)} %bitcast.14, s32[4,3]{1,0:T(4,128)} %kpoints.1, s32[3,8]{1,0:T(4,128)} %bitcast.15, f32[16]{0:T(128)} %constant.4.clone.roots, f32[1,60,2,120]{3,2,1,0:T(2,128)} %bitcast.12), custom_call_target="tpu_custom_call" | custom-call | tf_op jit(solution)/shard_map/pallas_call | solution.py:356
  47.0 2.2 %multiply_bitcast_fusion = f32[60,1,2,2,576]{4,3,2,1,0:T(2,128)} fusion(f32[60,2,2,576]{3,2,1,0:T(2,128)} %shard_map.82, f32[60]{0:T(128)S(1)} %rsqrt_bitcast_fusion), kind=kLoop, calls=%fused_computation | loop fusion | flops 138240 | bytes 1106160 | tf_op jit(solution)/shard_map/mul | solution.py:394
